TPU v7x, 256 devices: a whole 4x4x8 slice. The times are simulated.
256 devices in a mesh: row: 32 (over x, z), col: 8 (over y, core).
Axes of the slice: x: 4, y: 4, z: 8, core: 2. Of those that a mesh axis runs over, the one named last changes fastest.
Arguments:
- front: float32 [6, 32, 64, 12, 8, 128], P(None, 'row', None, None, 'col'), as said below
Outputs:
- factored: float32 [6, 32, 64, 12, 8, 128], P(None, 'row', None, None, 'col')
Inputs may be any that keep to these rules, and one draw needn't show every extreme that they name: `front`: read as A, the matrix is symmetric and positive definite.
All inputs are finite; a program needn't handle non-finite values.
Results may differ from a plain program's by a relative error of at most 0.0001.
Values sent between devices are 32-bit elements; how exact they have to be, the bound alone decides.
No kernel may reach another device: no remote copies, remote signals or barrier semaphores. Data moves between devices by JAX's collectives and lax.ppermute only.
A program may use at most 64 MiB of HBM per device.

v0:
```python
import jax
import jax.numpy as jnp
from jax import lax
from jax.sharding import PartitionSpec as P

CB = 128
PANELS = 2
SUB = 256
PANEL = 512


def broadcast(shard, axis, root):
    mine = lax.axis_index(axis) == root
    return lax.psum(jnp.where(mine, shard, jnp.zeros_like(shard)), axis)


def exact_dot(left, right):
    return jnp.dot(left, right, precision=lax.Precision.HIGHEST)


def dot_transposed(left, right):
    return lax.dot_general(left, right, (((1,), (1,)), ((), ())), precision=lax.Precision.HIGHEST)


def triangle(block):
    lower_f = jnp.linalg.cholesky(block)
    inverse = jax.scipy.linalg.solve_triangular(
        lower_f, jnp.eye(block.shape[0], dtype=jnp.float32), lower=True
    )
    return (lower_f, inverse)


def selector(row_ids, leading, count):
    wanted = leading + jnp.arange(count, dtype=jnp.int32)
    return (row_ids[None, :] == wanted[:, None]).astype(jnp.float32)


def column_factor(part, row_ids, leading, lower_f, inverse, chooser):
    below = (row_ids >= leading + SUB)[:, None]
    return jnp.where(below, dot_transposed(part, inverse), 0.0) + exact_dot(chooser.T, lower_f)


def fetch_panel(slab, first_block, col_devices):
    offset = first_block % col_devices
    whole = lax.all_gather(slab, "col", axis=1, tiled=True)
    return whole[:, offset * CB : (offset + 4) * CB]


def factor_panel(panel, row_ids, anchor):
    second = anchor + SUB
    chooser_first = selector(row_ids, anchor, SUB)
    chooser_second = selector(row_ids, second, SUB)
    pan_first = panel[:, :SUB]
    pan_second = panel[:, SUB:]
    pivot_a = lax.psum(exact_dot(chooser_first, pan_first), "row")
    lower_a, inverse_a = triangle(pivot_a)
    left_cols = column_factor(pan_first, row_ids, anchor, lower_a, inverse_a, chooser_first)
    crossing = lax.psum(exact_dot(chooser_second, left_cols), "row")
    pan_second = pan_second - dot_transposed(left_cols, crossing)
    pivot_b = lax.psum(exact_dot(chooser_second, pan_second), "row")
    lower_b, inverse_b = triangle(pivot_b)
    right_cols = column_factor(pan_second, row_ids, second, lower_b, inverse_b, chooser_second)
    return jnp.concatenate([left_cols, right_cols], axis=1)


def send_rows(lpanel, row_ranks, col_rank, col_devices, row_blocks):
    groups = row_ranks // (2 * col_devices)
    pieces = []
    for group in range(groups):
        for member in range(2):
            source = 2 * col_devices * group + 2 * col_rank + member
            pieces.append(broadcast(lpanel, "row", source))
    stacked = jnp.stack(pieces).reshape(groups, 2, row_blocks, lpanel.shape[0] // row_blocks, PANEL)
    return stacked.transpose(2, 0, 1, 3, 4).reshape(
        row_blocks * groups * 2 * (lpanel.shape[0] // row_blocks), PANEL
    )


def shards(front):
    row_blocks, _, row_tile, col_blocks, _, col_tile = front.shape
    row_devices = lax.axis_size("row")
    col_devices = lax.axis_size("col")
    row_rank = lax.axis_index("row")
    col_rank = lax.axis_index("col")
    local_rows = row_blocks * row_tile
    local_cols = col_blocks * col_tile
    local = front.reshape(local_rows, local_cols)
    row_ids = (
        (jnp.arange(row_blocks, dtype=jnp.int32)[:, None] * row_devices + row_rank) * row_tile
        + jnp.arange(row_tile, dtype=jnp.int32)[None, :]
    ).reshape(local_rows)
    col_ids = (
        (jnp.arange(col_blocks, dtype=jnp.int32)[:, None] * col_devices + col_rank) * col_tile
        + jnp.arange(col_tile, dtype=jnp.int32)[None, :]
    ).reshape(local_cols)
    for panel_index in range(PANELS):
        anchor = panel_index * PANEL
        first_block = 4 * panel_index
        slab_start = first_block // col_devices * CB
        panel = fetch_panel(local[:, slab_start : slab_start + CB], first_block, col_devices)
        lpanel = factor_panel(panel, row_ids, anchor)
        lcols = send_rows(lpanel, row_devices, col_rank, col_devices, row_blocks)
        local = local - dot_transposed(lpanel, lcols)
        position = col_rank - first_block % col_devices
        inside = (position >= 0) & (position < 4)
        taken = lax.dynamic_slice_in_dim(lpanel, jnp.clip(position, 0, 3) * CB, CB, 1)
        new_slab = jnp.where(inside, taken, local[:, slab_start : slab_start + CB])
        local = local.at[:, slab_start : slab_start + CB].set(new_slab)
    finished = PANELS * PANEL
    retain = (row_ids[:, None] >= finished) | (col_ids[None, :] < finished)
    local = jnp.where(retain, local, 0.0)
    return local.reshape(front.shape)


def solution(mesh):
    in_specs = (P(None, "row", None, None, "col", None),)
    out_specs = P(None, "row", None, None, "col", None)
    return jax.shard_map(shards, mesh=mesh, in_specs=in_specs, out_specs=out_specs, check_vma=False)
```

profile of v0, /device:TPU:8, one launch (start us, length us, event | category | flops | bytes accessed | tf_op | source)
XLA Modules:
  0.0 1581.4 jit_solution(15269130157193248069)
XLA Ops:
  6.5 7.3 reduce.17
  14.9 1.4 copy-done.1
  17.3 29.9 %all-gather.3.cloned.1.call-done = f32[384,1024]{1,0:T(8,128)} async-done(((f32[384,128]{1,0:T(8,128)}), f32[384,1024]{1,0:T(8,128)}) %all-gather.3.cloned.1.call-update) | async-done | bytes 1572880 | tf_op jit(solution)/shard_map/all_gather | solution.py:45
  47.2 2.2 fusion.14
  50.3 146.0 %all-reduce.12.cloned.1.call-done = f32[256,256]{0,1:T(8,128)} async-done(((f32[256,256]{0,1:T(8,128)}), f32[256,256]{0,1:T(8,128)}) %all-reduce.12.cloned.1.call-update) | async-done | bytes 262160 | tf_op jit(solution)/shard_map/psum | solution.py:55
  198.5 11.7 cholesky.214
  210.2 9.8 custom-call.17
  220.6 11.7 cholesky.231
  234.4 4.4 while.10
  235.5 1.3 bitcast_dynamic-update-slice_fusion.8
  237.4 1.3 bitcast_dynamic-update-slice_fusion.8
  238.8 19.7 %custom-call.18 = f32[2,128,128]{1,2,0:T(8,128)S(1)} custom-call(f32[2,128,128]{2,1,0:T(8,128)S(1)} %get-tuple-element.57), custom_call_target="InvertDiagBlocksLowerTriangular" | custom-call | tf_op jit(solution)/shard_map/jit(_solve_triangular)/triangular_solve | solution.py:27
  261.6 141.1 %all-reduce.14.cloned.1.call-done = f32[256,256]{1,0:T(8,128)} async-done(((f32[256,256]{1,0:T(8,128)}), f32[256,256]{1,0:T(8,128)}) %all-reduce.14.cloned.1.call-update) | async-done | bytes 262160 | tf_op jit(solution)/shard_map/psum | solution.py:58
  402.7 1.7 convolution_subtract_fusion.3
  405.8 141.3 %all-reduce.16.cloned.1.call-done = f32[256,256]{0,1:T(8,128)} async-done(((f32[256,256]{0,1:T(8,128)}), f32[256,256]{0,1:T(8,128)}) %all-reduce.16.cloned.1.call-update) | async-done | bytes 262160 | tf_op jit(solution)/shard_map/psum | solution.py:60
  549.1 11.7 cholesky.248
  560.9 9.8 custom-call.19
  571.2 11.7 cholesky.265
  585.6 4.2 while.11
  586.5 1.3 bitcast_dynamic-update-slice_fusion.9
  588.5 1.3 bitcast_dynamic-update-slice_fusion.9
  589.9 19.7 %custom-call.20 = f32[2,128,128]{1,2,0:T(8,128)S(1)} custom-call(f32[2,128,128]{2,1,0:T(8,128)S(1)} %get-tuple-element.58), custom_call_target="InvertDiagBlocksLowerTriangular" | custom-call | tf_op jit(solution)/shard_map/jit(_solve_triangular)/triangular_solve | solution.py:27
  611.5 1.7 select_bitcast_fusion.7
  613.3 1.6 copy-done.2
  614.9 1.9 copy.22
  617.6 151.1 %all-reduce.26.cloned.1.call-done = (f32[1,384,512]{1,2,0:T(8,128)}, f32[1,384,512]{1,2,0:T(8,128)}, f32[1,384,512]{1,2,0:T(8,128)}, f32[1,384,512]{1,2,0:T(8,128)}) async-done(((f32[1,384,512]{1,2,0:T(8,128)}, f32[1,384,512]{1,2,0:T(8,128)}, f32[1,384,512]{1,2,0:T(8,128)}, f32[1,384,512]{1,2,0:T(8,128)}), (f32[1,384,512]{1,2,0:T(8,128)}, f32[1,384,512]{1,2,0:T(8,128)}, f32[1,384,512]{1,2,0:T(8,128)}, ...) | async-done | bytes 3145744 | tf_op jit(solution)/shard_map/psum | solution.py:14
  768.6 3.7 pad_maximum_fusion
  772.4 3.6 copy.20
  775.9 2.3 copy.21
  778.6 5.2 convolution_subtract_fusion.1
  783.8 1.3 select_select_fusion.1
  785.2 22.8 %all-gather.5.cloned.1.call-done = f32[384,1024]{0,1:T(8,128)} async-done(((f32[384,128]{0,1:T(8,128)}), f32[384,1024]{0,1:T(8,128)}) %all-gather.5.cloned.1.call-update) | async-done | bytes 1572880 | tf_op jit(solution)/shard_map/all_gather | solution.py:45
  808.0 2.2 fusion.12
  810.7 146.9 %all-reduce.18.cloned.1.call-done = f32[256,256]{0,1:T(8,128)} async-done(((f32[256,256]{0,1:T(8,128)}), f32[256,256]{0,1:T(8,128)}) %all-reduce.18.cloned.1.call-update) | async-done | bytes 262160 | tf_op jit(solution)/shard_map/psum | solution.py:55
  959.7 11.7 cholesky.282
  971.5 9.8 custom-call.21
  981.8 11.7 cholesky.299
  996.1 5.1 while.12
  997.3 1.3 bitcast_dynamic-update-slice_fusion.10
  999.9 1.3 bitcast_dynamic-update-slice_fusion.10
  1001.3 19.7 %custom-call.22 = f32[2,128,128]{1,2,0:T(8,128)S(1)} custom-call(f32[2,128,128]{2,1,0:T(8,128)S(1)} %get-tuple-element.59), custom_call_target="InvertDiagBlocksLowerTriangular" | custom-call | tf_op jit(solution)/shard_map/jit(_solve_triangular)/triangular_solve | solution.py:27
  1021.9 1.6 convolution_select_fusion.1
  1025.2 141.2 %all-reduce.20.cloned.1.call-done = f32[256,256]{1,0:T(8,128)} async-done(((f32[256,256]{1,0:T(8,128)}), f32[256,256]{1,0:T(8,128)}) %all-reduce.20.cloned.1.call-update) | async-done | bytes 262160 | tf_op jit(solution)/shard_map/psum | solution.py:58
  1166.4 1.7 convolution_subtract_fusion.2
  1169.5 141.8 %all-reduce.22.cloned.1.call-done = f32[256,256]{0,1:T(8,128)} async-done(((f32[256,256]{0,1:T(8,128)}), f32[256,256]{0,1:T(8,128)}) %all-reduce.22.cloned.1.call-update) | async-done | bytes 262160 | tf_op jit(solution)/shard_map/psum | solution.py:60
  1311.3 1.8 copy.28
  1314.8 11.7 cholesky.316
  1327.3 9.8 custom-call.23
  1337.1 1.7 constant_dynamic-update-slice_fusion
  1339.9 11.7 cholesky.333
  1354.9 1.7 fusion.35
  1356.5 7.2 while.13
  1358.0 2.3 bitcast_dynamic-update-slice_fusion.11
  1361.6 2.2 bitcast_dynamic-update-slice_fusion.11
  1364.4 20.5 %custom-call.24 = f32[2,128,128]{1,2,0:T(8,128)S(1)} custom-call(f32[2,128,128]{2,1,0:T(8,128)} %copy-done.6), custom_call_target="InvertDiagBlocksLowerTriangular" | custom-call | tf_op jit(solution)/shard_map/jit(_solve_triangular)/triangular_solve | solution.py:27
  1387.3 1.4 convolution_add_fusion
  1388.7 1.7 select_bitcast_fusion.3
  1391.4 154.5 %all-reduce.24.cloned.1.call-done = (f32[1,384,512]{1,2,0:T(8,128)}, f32[1,384,512]{1,2,0:T(8,128)}, f32[1,384,512]{1,2,0:T(8,128)}, f32[1,384,512]{1,2,0:T(8,128)}) async-done(((f32[1,384,512]{1,2,0:T(8,128)}, f32[1,384,512]{1,2,0:T(8,128)}, f32[1,384,512]{1,2,0:T(8,128)}, f32[1,384,512]{1,2,0:T(8,128)}), (f32[1,384,512]{1,2,0:T(8,128)}, f32[1,384,512]{1,2,0:T(8,128)}, f32[1,384,512]{1,2,0:T(8,128)}, ...) | async-done | bytes 3145744 | tf_op jit(solution)/shard_map/psum | solution.py:14
  1545.9 3.7 pad_maximum_fusion.1
  1549.6 3.6 copy.29
  1553.2 2.2 copy.30
  1555.4 5.3 convolution_subtract_fusion
  1561.7 3.5 reshape.217
  1565.3 9.1 copy.33
  (134 shorter events, 44.3 us)
Async XLA Ops:
  6.5 40.7 %all-gather.3.cloned.1.call-start = ((), (), s32[]{:S(2)}) async-start(), calls=%async_computation | async-start | bytes 1769472 | tf_op jit(solution)/shard_map/all_gather | solution.py:45
  14.9 1.4 copy-start.1
  17.1 179.2 %all-reduce.12.cloned.1.call-start = ((), (), s32[]{:S(2)}) async-start(), calls=%async_computation.1 | async-start | bytes 524288 | tf_op jit(solution)/shard_map/psum | solution.py:55
  49.5 353.2 %all-reduce.14.cloned.1.call-start = ((), (), s32[]{:S(2)}) async-start(), calls=%async_computation.2 | async-start | bytes 524288 | tf_op jit(solution)/shard_map/psum | solution.py:58
  197.4 62.0 %copy-start.4 = (f32[384,1024]{1,0:T(8,128)S(1)}, f32[384,1024]{1,0:T(8,128)}, u32[]{:S(2)}) copy-start(f32[384,1024]{1,0:T(8,128)} %all-gather.3.cloned.1.call-done) | copy-start | bytes 4718596
  261.6 285.5 %all-reduce.16.cloned.1.call-start = ((), (), s32[]{:S(2)}) async-start(), calls=%async_computation.3 | async-start | bytes 524288 | tf_op jit(solution)/shard_map/psum | solution.py:60
  405.7 362.9 %all-reduce.26.cloned.1.call-start = ((), (), s32[]{:S(2)}) async-start(), calls=%async_computation.9 | async-start | bytes 6291456 | tf_op jit(solution)/shard_map/psum | solution.py:14
  589.9 23.4 %copy-start.7 = (s32[2,2]{1,0:T(2,128)}, s32[2,2]{1,0:T(2,128)S(1)}, u32[]{:S(2)}) copy-start(s32[2,2]{1,0:T(2,128)S(1)} %get-tuple-element.396) | copy-start | bytes 52
  613.2 1.7 copy-start.2
  613.3 194.7 %all-gather.5.cloned.1.call-start = ((), (), s32[]{:S(2)}) async-start(), calls=%async_computation.4 | async-start | bytes 1769472 | tf_op jit(solution)/shard_map/all_gather | solution.py:45
  775.9 2.6 copy-start
  785.1 172.5 %all-reduce.18.cloned.1.call-start = ((), (), s32[]{:S(2)}) async-start(), calls=%async_computation.5 | async-start | bytes 524288 | tf_op jit(solution)/shard_map/psum | solution.py:55
  810.2 356.1 %all-reduce.20.cloned.1.call-start = ((), (), s32[]{:S(2)}) async-start(), calls=%async_computation.6 | async-start | bytes 524288 | tf_op jit(solution)/shard_map/psum | solution.py:58
  1025.1 286.1 %all-reduce.22.cloned.1.call-start = ((), (), s32[]{:S(2)}) async-start(), calls=%async_computation.7 | async-start | bytes 524288 | tf_op jit(solution)/shard_map/psum | solution.py:60
  1169.3 376.6 %all-reduce.24.cloned.1.call-start = ((), (), s32[]{:S(2)}) async-start(), calls=%async_computation.8 | async-start | bytes 6291456 | tf_op jit(solution)/shard_map/psum | solution.py:14
  1314.1 0.7 copy-start.5
  1363.8 0.7 copy-start.6
  1390.5 0.9 copy-start.3
Sparse Core Ops, SparseCore 0:
  17.2 30.0 all-gather.2
  50.7 145.5 all-reduce.11
  261.7 140.9 all-reduce.13
  406.0 141.0 all-reduce.15
  613.4 155.2 all-reduce.25
  785.3 22.7 all-gather.4
  811.9 145.7 all-reduce.17
  1025.3 141.0 all-reduce.19
  1170.2 141.0 all-reduce.21
  1390.6 155.2 all-reduce.23
where the time goes:
time: 1590 us; the launch traced here: 1580 us
  waiting for transfers between devices  1220 us (77%)
  other arithmetic  246 us (15%)
  local copies, waits for them, and re-layouts  59.4 us (4%)
  matrix products  37.9 us (2%)
  between operations  19.4 us (1%)
    psum x2, waiting for transfers between devices, broadcast(): return lax.psum(jnp.where(mine, shard, jnp.zeros_like(shard)), axis)  306 us
    psum x2, waiting for transfers between devices, factor_panel(): pivot_a = lax.psum(exact_dot(chooser_first, pan_first), 'row')  293 us
    psum x2, waiting for transfers between devices, factor_panel(): pivot_b = lax.psum(exact_dot(chooser_second, pan_second), 'row')  283 us
    psum x2, waiting for transfers between devices, factor_panel(): crossing = lax.psum(exact_dot(chooser_second, left_cols), 'row')  282 us
    another operation x27, other arithmetic, triangle(): lower_f = jnp.linalg.cholesky(block)  139 us
    another operation x9, other arithmetic, triangle(): jax.scipy.linalg.solve_triangular(lower_f, jnp.eye(block.shape[0], dtype=...  81.3 us
    all_gather x2, waiting for transfers between devices, fetch_panel(): whole = lax.all_gather(slab, 'col', axis=1, tiled=True)  52.7 us
  transfers between devices with their start and end apart: 10, of which 10 were waited for; matrix products, arithmetic and copies ran while one was open for 0% of the time, Pallas kernels for 0%

commit v1 on v0

v1 whole, which is shorter than its diff:
```python
import functools

import jax
import jax.numpy as jnp
from jax import lax
from jax.experimental import pallas as pl
from jax.experimental.pallas import tpu as pltpu
from jax.sharding import PartitionSpec as P

B = 128
HALF = 512
FULL = 1024
F32 = jnp.float32
BF16 = jnp.bfloat16
VMEM = pl.BlockSpec(memory_space=pltpu.VMEM)
SMEM = pl.BlockSpec(memory_space=pltpu.SMEM)
LIMIT = 56 * 1024 * 1024


def lane(tile, c):
    return jnp.broadcast_to(tile[:, c : c + 1], (8, B))


def sub(tile, i):
    return jnp.broadcast_to(tile[i : i + 1, :], (8, B))


def exact(left, right, dims):
    return lax.dot_general(
        left, right, (dims, ((), ())), precision=lax.Precision.HIGHEST, preferred_element_type=F32
    )


def split(value):
    high = value.astype(BF16)
    return high, (value - high.astype(F32)).astype(BF16)


def dot3(left, right, dims):
    mul = lambda a, b: lax.dot_general(a, b, (dims, ((), ())), preferred_element_type=F32)
    return mul(left[0], right[0]) + (mul(left[0], right[1]) + mul(left[1], right[0]))


def factor_block(rows):
    rows = list(rows)
    col = lax.broadcasted_iota(jnp.int32, (8, B), 1)
    row = lax.broadcasted_iota(jnp.int32, (8, B), 0)
    uppers, inverses = [], []
    for p in range(16):
        top = rows[p]
        o = 8 * p
        inside = (col >= o) & (col < o + 8)
        cols = [lane(top, o + j) for j in range(8)]
        a = {(i, j): sub(cols[j], i) for j in range(8) for i in range(j, 8)}
        unit = jnp.where(inside, (col - o == row).astype(F32), top)
        m, inv = {}, []
        for j in range(8):
            rcp = 1.0 / a[j, j]
            inv.append(rcp)
            for i in range(j + 1, 8):
                m[i, j] = a[i, j] * rcp
            for k in range(j + 1, 8):
                for i in range(k, 8):
                    a[i, k] = a[i, k] - m[i, j] * a[k, j]
        n = {}
        for j in range(8):
            for i in range(j + 1, 8):
                acc = m[i, j]
                for k in range(j + 1, i):
                    acc = acc + m[i, k] * n[k, j]
                n[i, j] = -acc
        spread = [sub(unit, j) for j in range(8)]
        z = []
        for i in range(8):
            acc = spread[i]
            for k in range(i):
                acc = acc + n[i, k] * spread[k]
            z.append(acc)
        scaled = [z[i] * inv[i] for i in range(8)]
        v = []
        for j in range(8):
            acc = scaled[j]
            for i in range(j + 1, 8):
                acc = acc + n[i, j] * scaled[i]
            v.append(acc)
        for q in range(p + 1, 16):
            t = [lane(rows[q], o + j) * v[j] for j in range(8)]
            s = ((t[0] + t[1]) + (t[2] + t[3])) + ((t[4] + t[5]) + (t[6] + t[7]))
            rows[q] = jnp.where(inside, 0.0, rows[q]) - s
        roots = [lax.rsqrt(a[j, j]) for j in range(8)]
        w = z[0] * roots[0]
        for i in range(1, 8):
            w = jnp.where(row == i, z[i] * roots[i], w)
        u = w
        for i in range(8):
            root = a[i, i] * roots[i]
            u = jnp.where((row == i) & (col == o + i), root, u)
            for j in range(i + 1, 8):
                u = jnp.where((row == i) & (col == o + j), root * m[j, i], u)
        uppers.append(jnp.where(col >= o + row, u, 0.0))
        inverses.append(jnp.where(col <= o + row, w, 0.0))
    return uppers, inverses


def factor_half(s_ref, u_ref, w_ref):
    blocks = HALF // B

    @pl.loop(0, blocks)
    def _(k):
        o = pl.multiple_of(k * B, B)
        here = pl.ds(o, B)
        tiles = [s_ref[pl.ds(pl.multiple_of(o + 8 * i, 8), 8), here] for i in range(16)]
        uppers, inverses = factor_block(tiles)
        u_diag = jnp.concatenate(uppers, axis=0)
        w_diag = jnp.concatenate(inverses, axis=0)
        s_ref[here, here] = jnp.eye(B, dtype=F32)
        made = exact(w_diag, s_ref[here, :], ((1,), (0,)))
        s_ref[here, :] = made
        block = lax.broadcasted_iota(jnp.int32, (B, HALF), 1) // B
        u_ref[here, :] = jnp.where(block > k, made, 0.0)
        w_ref[here, :] = jnp.where(block <= k, made, 0.0)
        u_ref[here, here] = u_diag

        @pl.loop(k + 1, blocks)
        def _(i):
            there = pl.ds(pl.multiple_of(i * B, B), B)
            mult = s_ref[here, there]
            s_ref[there, here] = jnp.zeros((B, B), F32)
            s_ref[there, :] = s_ref[there, :] - exact(mult, made, ((0,), (0,)))


def place(where_ref, own_ref, other_ref, dst_ref, count):
    z4 = where_ref[1] & 3
    core = where_ref[3]
    for s in range(4):
        for h in range(2):
            for y in range(count):
                r = pl.ds(pl.multiple_of(h * 256 + (z4 ^ s) * 64, 64), 64)
                dst_ref[r, pl.ds(pl.multiple_of(y * 256 + core * B, B), B)] = own_ref[s, h, y]
                dst_ref[r, pl.ds(pl.multiple_of(y * 256 + (1 - core) * B, B), B)] = other_ref[s, h, y]


def first_kernel(where_ref, own_ref, other_ref, u_ref, w_ref, s_ref):
    place(where_ref, own_ref, other_ref, s_ref, 2)
    factor_half(s_ref, u_ref, w_ref)


def first_half(where, own, other):
    shape = jax.ShapeDtypeStruct((HALF, HALF), F32)
    return pl.pallas_call(
        first_kernel,
        out_shape=(shape, shape),
        in_specs=[SMEM, VMEM, VMEM],
        out_specs=(VMEM, VMEM),
        scratch_shapes=[pltpu.VMEM((HALF, HALF), F32)],
        compiler_params=pltpu.CompilerParams(vmem_limit_bytes=LIMIT),
        name="first_half",
    )(where, own, other)


def second_kernel(where_ref, own_ref, other_ref, ua_ref, wa_ref, u_ref, w_ref, raw_ref, s_ref, ub_ref, wb_ref):
    place(where_ref, own_ref, other_ref, raw_ref, 4)
    cross = exact(wa_ref[...], raw_ref[:, :HALF], ((1,), (1,)))
    u_ref[:HALF, HALF:] = cross
    s_ref[...] = raw_ref[:, HALF:] - exact(cross, cross, ((0,), (0,)))
    factor_half(s_ref, ub_ref, wb_ref)
    u_ref[:HALF, :HALF] = ua_ref[...]
    u_ref[HALF:, :HALF] = jnp.zeros((HALF, HALF), F32)
    u_ref[HALF:, HALF:] = ub_ref[...]
    w_ref[:HALF, :HALF] = wa_ref[...]
    w_ref[:HALF, HALF:] = jnp.zeros((HALF, HALF), F32)
    w_ref[HALF:, HALF:] = wb_ref[...]
    part = exact(u_ref[:HALF, HALF:], wa_ref[...], ((0,), (0,)))
    w_ref[HALF:, :HALF] = -exact(wb_ref[...], part, ((1,), (0,)))


def second_half(where, own, other, ua, wa):
    shape = jax.ShapeDtypeStruct((FULL, FULL), F32)
    half = pltpu.VMEM((HALF, HALF), F32)
    return pl.pallas_call(
        second_kernel,
        out_shape=(shape, shape),
        in_specs=[SMEM] + [VMEM] * 4,
        out_specs=(VMEM, VMEM),
        scratch_shapes=[pltpu.VMEM((HALF, FULL), F32), half, half, half],
        compiler_params=pltpu.CompilerParams(vmem_limit_bytes=LIMIT),
        name="second_half",
    )(where, own, other, ua, wa)


def rows_kernel(where_ref, own_ref, other_ref, u_ref, w_ref, high_ref, low_ref, slab_ref, a_ref, x_ref):
    y = where_ref[2]
    core = where_ref[3]
    for s in range(4):
        base = ((y - s) & 3) * 256
        a_ref[:, pl.ds(pl.multiple_of(base + core * B, B), B)] = own_ref[s]
        a_ref[:, pl.ds(pl.multiple_of(base + (1 - core) * B, B), B)] = other_ref[s]
    step = 256
    for k in range(0, FULL, step):
        x_ref[:, k : k + step] = dot3(
            split(a_ref[:, : k + step]), split(w_ref[k : k + step, : k + step]), ((1,), (1,))
        )
    for j in range(0, FULL, step):
        value = dot3(split(x_ref[:, j:]), split(w_ref[j:, j : j + step]), ((1,), (0,)))
        high, low = split(value)
        high_ref[:, j : j + step] = high
        low_ref[:, j : j + step] = low
    row_rank = where_ref[0] * 8 + where_ref[1]
    mine = pl.ds(pl.multiple_of((y * 2 + core) * B, B), B)
    slab_ref[...] = x_ref[:, mine]

    @pl.when(row_rank < 16)
    def _():
        block = u_ref[mine, pl.ds(pl.multiple_of((row_rank // 2) * B, B), B)].T
        slab_ref[:64, :] = jnp.where(row_rank % 2 == 0, block[:64], block[64:])


def row_factor(where, own, other, u, w):
    rows = own.shape[1]
    return pl.pallas_call(
        rows_kernel,
        out_shape=(
            jax.ShapeDtypeStruct((rows, FULL), BF16),
            jax.ShapeDtypeStruct((rows, FULL), BF16),
            jax.ShapeDtypeStruct((rows, B), F32),
        ),
        in_specs=[SMEM] + [VMEM] * 4,
        out_specs=(VMEM, VMEM, VMEM),
        scratch_shapes=[pltpu.VMEM((rows, FULL), F32), pltpu.VMEM((rows, FULL), F32)],
        compiler_params=pltpu.CompilerParams(vmem_limit_bytes=LIMIT),
        name="row_factor",
    )(where, own, other, u, w)


def trailing_kernel(where_ref, a_ref, bulk_ref, high_ref, low_ref, slab_ref, out_ref, bh_ref, bl_ref):
    rows = high_ref.shape[0]
    blocks = a_ref.shape[0] // rows
    row_rank = where_ref[0] * 8 + where_ref[1]
    gone = (row_rank < 16) & (lax.broadcasted_iota(jnp.int32, (rows, B), 0) < 64)

    def load(d, at):
        for p in range(2):
            for z in range(8):
                for part in range(2):
                    if part == 0:
                        source = 8 * p + z
                    else:
                        source = (24 if p == 0 else 16) + z
                    piece = bulk_ref[source, pl.ds(d, 32, stride=blocks), :]
                    high, low = split(piece)
                    r = HALF * p + 64 * z + 32 * part
                    bh_ref[r : r + 32, at : at + B] = high
                    bl_ref[r : r + 32, at : at + B] = low

    @pl.loop(0, blocks // 2)
    def _(pair):
        load(2 * pair, 0)
        load(2 * pair + 1, B)
        made = dot3((high_ref[...], low_ref[...]), (bh_ref[...], bl_ref[...]), ((1,), (0,)))
        for t in range(2):
            at = pl.ds(2 * pair + t, rows, stride=blocks)
            value = a_ref[at, :] - made[:, t * B : (t + 1) * B]
            out_ref[at, :] = jnp.where(gone, 0.0, value)

    out_ref[pl.ds(0, rows, stride=blocks), :] = slab_ref[...]


def trailing(where, a, bulk, high, low, slab):
    return pl.pallas_call(
        trailing_kernel,
        out_shape=jax.ShapeDtypeStruct(a.shape, F32),
        in_specs=[SMEM] + [VMEM] * 5,
        out_specs=VMEM,
        scratch_shapes=[pltpu.VMEM((FULL, 2 * B), BF16), pltpu.VMEM((FULL, 2 * B), BF16)],
        compiler_params=pltpu.CompilerParams(vmem_limit_bytes=LIMIT),
        name="trailing",
    )(where, a, bulk, high, low, slab)


def row_pairs(f):
    return [(x * 8 + z, (f(x, z)[0] % 4) * 8 + f(x, z)[1] % 8) for x in range(4) for z in range(8)]


def col_shift(s):
    return [(c, (c + 2 * s) % 8) for c in range(8)]


def swap_core(value):
    return lax.ppermute(value, "col", [(c, c ^ 1) for c in range(8)])


def from_x(source, target):
    return [(source * 8 + z, target * 8 + z) for z in range(8)]


def shards(front):
    lin = front.reshape(-1, B)
    rows = 384
    r = lax.axis_index("row")
    c = lax.axis_index("col")
    x, z, y, core = r // 8, r % 8, c // 2, c % 2
    where = jnp.stack([x, z, y, core]).astype(jnp.int32)

    slab = lax.slice(lin, (0, 0), lin.shape, (lin.shape[0] // rows, 1))
    piece = slab[:64]
    near = [piece] + [lax.ppermute(piece, "col", col_shift(s)) for s in (3, 2, 1)]
    ring = jnp.stack(near + near[:3])
    mine = lax.dynamic_slice_in_dim(ring, (4 - y) % 4, 4, 0)

    top = lin[:768]
    moved = lax.ppermute(top[384:], "row", from_x(0, 3) + from_x(1, 2))
    bulk = lax.all_gather(jnp.where(x >= 2, moved, top[:384]), "row", axis=0)

    across = lax.ppermute(mine, "row", row_pairs(lambda x, z: (x, z + 4)))
    both = jnp.where(z < 4, jnp.stack([mine, across]), jnp.stack([across, mine]))

    def broadcast_x(value, source):
        got = [lax.ppermute(value, "row", from_x(source, t)) for t in range(4) if t != source]
        out = value
        for t, g in zip([t for t in range(4) if t != source], got):
            out = jnp.where(x == t, g, out)
        return out

    def gather_z4(value):
        return jnp.stack(
            [value] + [lax.ppermute(value, "row", row_pairs(lambda x, z: (x, z ^ s))) for s in (1, 2, 3)]
        )

    part_a = gather_z4(broadcast_x(both[:, :2], 0))
    part_b = gather_z4(broadcast_x(both, 1))
    ua, wa = first_half(where, part_a, swap_core(part_a))
    u, w = second_half(where, part_b, swap_core(part_b), ua, wa)

    wide = jnp.stack([slab] + [lax.ppermute(slab, "col", col_shift(s)) for s in (1, 2, 3)])
    high, low, own_slab = row_factor(where, wide, swap_core(wide), u, w)
    out = trailing(where, lin, bulk, high, low, own_slab)
    return out.reshape(front.shape)


def solution(mesh):
    spec = P(None, "row", None, None, "col", None)
    return jax.shard_map(shards, mesh=mesh, in_specs=(spec,), out_specs=spec, check_vma=False)
```

time: 1590 us -> 205 us (0.13)
  waiting for transfers between devices: 1220 us -> 52 us
  other arithmetic: 246 us -> 2.77 us
  Pallas kernels: 0 us -> 84.2 us
  local copies, waits for them, and re-layouts: 59.4 us -> 3.78 us
  starting transfers between devices: 1.13 us -> 45.8 us
  matrix products: 37.9 us -> 0 us
    psum x8 -> x0, waiting for transfers between devices: 1160 us -> none  [the longest x2 306 us: broadcast(): return lax.psum(jnp.where(mine, shard, jnp.zeros_like(shard)), axis)]
    another operation x41 -> x4, other arithmetic: 231 us -> 1.95 us  [the longest x1 1.17 us: shards(): jnp.stack([slab] + [lax.ppermute(slab, 'col', col_shift(s)) for s in (1,...]
    pallas_call x0 -> x4, Pallas kernels: none -> 84.2 us  [the longest x1 37.7 us: second_half(): pl.pallas_call(second_kernel, out_shape=(shape, shape), in_specs=[SMEM] +...]
    all_gather x2 -> x1, waiting for transfers between devices: 52.7 us -> 0.01 us  [shards(): bulk = lax.all_gather(jnp.where(x >= 2, moved, top[:384]), 'row', axis=0)]
    ppermute x0 -> x23, waiting for transfers between devices: none -> 52 us  [the longest x6 24.9 us: gather_z4(): lax.ppermute(value, 'row', row_pairs(lambda x, z: (x, z ^ s)))]
    ppermute x0 -> x23, starting transfers between devices: none -> 45.8 us  [the longest x6 12.9 us: broadcast_x(): lax.ppermute(value, 'row', from_x(source, t))]
    dot_general x18 -> x0, matrix products: 29.3 us -> none  [the longest x8 17.4 us: dot_transposed(): lax.dot_general(left, right, (((1,), (1,)), ((), ())), precision=lax.Prec...]
    another operation x39 -> x2, local copies, waits for them, and re-layouts: 28.1 us -> 0.01 us  [the longest x1 0.01 us: shards(): jnp.stack([mine, across])]
  transfers between devices with their start and end apart: 10 -> 24, of which waited for: 10 -> 14; matrix products, arithmetic and copies ran while one was open for 0% -> 2% of each run, Pallas kernels for 0% -> 36%
where the time goes in v1:
time: 205 us; the launch traced here: 202 us
  Pallas kernels  84.2 us (41%)
  waiting for transfers between devices  52 us (25%)
  starting transfers between devices  45.8 us (22%)
  between operations  13.7 us (7%)
  local copies, waits for them, and re-layouts  3.78 us (2%)
  other arithmetic  2.77 us (1%)
    pallas_call x1, Pallas kernels, second_half(): pl.pallas_call(second_kernel, out_shape=(shape, shape), in_specs=[SMEM] +...  37.7 us
    pallas_call x1, Pallas kernels, first_half(): pl.pallas_call(first_kernel, out_shape=(shape, shape), in_specs=[SMEM, VM...  26.9 us
    ppermute x6, waiting for transfers between devices, gather_z4(): lax.ppermute(value, 'row', row_pairs(lambda x, z: (x, z ^ s)))  24.9 us
    ppermute x6, waiting for transfers between devices, broadcast_x(): lax.ppermute(value, 'row', from_x(source, t))  15.2 us
    ppermute x6, starting transfers between devices, broadcast_x(): lax.ppermute(value, 'row', from_x(source, t))  12.9 us
    pallas_call x1, Pallas kernels, trailing(): pl.pallas_call(trailing_kernel, out_shape=jax.ShapeDtypeStruct(a.shape, F...  10.5 us
    ppermute x6, starting transfers between devices, gather_z4(): lax.ppermute(value, 'row', row_pairs(lambda x, z: (x, z ^ s)))  9.13 us
    pallas_call x1, Pallas kernels, row_factor(): pl.pallas_call(rows_kernel, out_shape=(jax.ShapeDtypeStruct((rows, FULL),...  9.12 us
  transfers between devices with their start and end apart: 24, of which 14 were waited for; matrix products, arithmetic and copies ran while one was open for 2% of the time, Pallas kernels for 36%

profile of v1, /device:TPU:8, one launch (start us, length us, event | category | flops | bytes accessed | tf_op | source)
XLA Modules:
  0.0 202.2 jit_solution(7750189669447591171)
XLA Ops:
  6.5 0.0 all-gather.3.cloned.1.call-start
  6.5 1.1 fusion
  7.6 4.7 %collective-permute-start = (f32[384,128]{1,0:T(8,128)S(1)}, f32[384,128]{1,0:T(8,128)S(1)}, u32[]{:S(2)}, u32[]{:S(2)}) collective-permute-start(f32[384,128]{1,0:T(8,128)S(1)} %bitcast.47), channel_id=1, source_target_pairs={{0,192},{8,200},{16,208},{24,216},{32,224},{40,232},{48,240},{56,2... | collective-permute-start | bytes 589832 | tf_op jit(solution)/shard_map/ppermute | solution.py:311
  12.3 4.1 %collective-permute-done = f32[384,128]{1,0:T(8,128)S(1)} collective-permute-done((f32[384,128]{1,0:T(8,128)S(1)}, f32[384,128]{1,0:T(8,128)S(1)}, u32[]{:S(2)}, u32[]{:S(2)}) %collective-permute-start) | collective-permute-done | bytes 196640 | tf_op jit(solution)/shard_map/ppermute | solution.py:311
  16.4 0.7 broadcast_select_fusion
  17.1 0.0 all-gather.3.cloned.1.call-update
  17.1 1.7 slice.29
  18.8 0.5 collective-permute-start.5
  19.4 2.6 %collective-permute-start.6 = (f32[64,128]{1,0:T(8,128)S(1)}, f32[64,128]{1,0:T(8,128)S(1)}, u32[]{:S(2)}, u32[]{:S(2)}) collective-permute-start(f32[64,128]{1,0:T(8,128)S(1)} %slice.32), channel_id=1, source_target_pairs={{0,4},{1,5},{2,6},{3,7},{4,0},{5,1},{6,2},{7,3},{8,12},{9,13},{10,... | collective-permute-start | bytes 98312 | tf_op jit(solution)/shard_map/ppermute | solution.py:306
  21.9 1.9 collective-permute-start.7
  23.8 0.0 collective-permute-done.5
  23.8 0.9 collective-permute-done.6
  24.8 1.1 collective-permute-done.7
  25.9 7.3 %collective-permute-start.8 = (f32[4,64,128]{2,1,0:T(8,128)S(1)}, f32[4,64,128]{2,1,0:T(8,128)S(1)}, u32[]{:S(2)}, u32[]{:S(2)}) collective-permute-start(f32[4,64,128]{2,1,0:T(8,128)S(1)} %constant_dynamic-slice_fusion), channel_id=1, source_target_pairs={{0,32},{8,40},{16,48},{24,56},{32,0},{40,8},{48,16},{56,24},{64,96... | collective-permute-start | bytes 393224 | tf_op jit(solution)/shard_map/ppermute | solution.py:314
  33.2 4.3 %collective-permute-done.8 = f32[4,64,128]{2,1,0:T(8,128)S(1)} collective-permute-done((f32[4,64,128]{2,1,0:T(8,128)S(1)}, f32[4,64,128]{2,1,0:T(8,128)S(1)}, u32[]{:S(2)}, u32[]{:S(2)}) %collective-permute-start.8) | collective-permute-done | bytes 131104 | tf_op jit(solution)/shard_map/ppermute | solution.py:314
  37.6 0.7 collective-permute-start.10
  38.3 1.3 collective-permute-start.11
  39.6 0.7 collective-permute-start.9
  40.3 0.0 collective-permute-done.10
  40.3 9.1 %collective-permute-done.11 = f32[2,4,64,128]{3,2,1,0:T(8,128)S(1)} collective-permute-done((f32[2,4,64,128]{3,2,1,0:T(8,128)S(1)}, f32[2,4,64,128]{3,2,1,0:T(8,128)S(1)}, u32[]{:S(2)}, u32[]{:S(2)}) %collective-permute-start.11) | collective-permute-done | bytes 262176 | tf_op jit(solution)/shard_map/ppermute | solution.py:318
  49.3 0.0 collective-permute-done.9
  49.4 0.1 select_select_fusion
  49.4 1.1 collective-permute-start.12
  50.6 2.7 %collective-permute-start.13 = (f32[2,4,64,128]{3,2,1,0:T(8,128)S(1)}, f32[2,4,64,128]{3,2,1,0:T(8,128)S(1)}, u32[]{:S(2)}, u32[]{:S(2)}) collective-permute-start(f32[2,4,64,128]{3,2,1,0:T(8,128)S(1)} %select_select_fusion), channel_id=1, source_target_pairs={{0,16},{8,24},{16,0},{24,8},{32,48},{40,56},{48,32},{56,40},{64,80... | collective-permute-start | bytes 786440 | tf_op jit(solution)/shard_map/ppermute | solution.py:326
  53.3 0.8 collective-permute-start.14
  54.1 2.0 collective-permute-start.2
  56.0 2.0 collective-permute-start.3
  58.0 1.1 collective-permute-done.12
  59.2 1.9 collective-permute-start.1
  61.1 10.3 %collective-permute-done.13 = f32[2,4,64,128]{3,2,1,0:T(8,128)S(1)} collective-permute-done((f32[2,4,64,128]{3,2,1,0:T(8,128)S(1)}, f32[2,4,64,128]{3,2,1,0:T(8,128)S(1)}, u32[]{:S(2)}, u32[]{:S(2)}) %collective-permute-start.13) | collective-permute-done | bytes 262176 | tf_op jit(solution)/shard_map/ppermute | solution.py:326
  71.4 7.6 %collective-permute-start.16 = (f32[2,2,64,128]{3,2,1,0:T(8,128)S(1)}, f32[2,2,64,128]{3,2,1,0:T(8,128)S(1)}, u32[]{:S(2)}, u32[]{:S(2)}) collective-permute-start(f32[2,2,64,128]{3,2,1,0:T(8,128)S(1)} %slice.33), channel_id=1, source_target_pairs={{0,192},{8,200},{16,208},{24,216},{32,224},{40,232},{48,240},{56,2... | collective-permute-start | bytes 393224 | tf_op jit(solution)/shard_map/ppermute | solution.py:318
  79.0 0.0 collective-permute-done.14
  79.0 1.3 collective-permute-start.17
  80.3 0.1 pad_maximum_fusion.own_ref
  80.5 0.0 copy-start
  80.5 0.0 collective-permute-done.2
  80.5 1.3 collective-permute-start.18
  81.8 0.0 collective-permute-done.3
  81.8 0.1 collective-permute-start.15
  81.9 0.0 collective-permute-done.1
  81.9 1.2 pad_maximum_fusion.1.own_ref
  83.1 0.0 copy-start.1
  83.1 0.6 collective-permute-start.4
  83.7 0.6 collective-permute-done.16
  84.2 1.4 collective-permute-done.17
  85.6 4.2 %collective-permute-done.18 = f32[2,2,64,128]{3,2,1,0:T(8,128)S(1)} collective-permute-done((f32[2,2,64,128]{3,2,1,0:T(8,128)S(1)}, f32[2,2,64,128]{3,2,1,0:T(8,128)S(1)}, u32[]{:S(2)}, u32[]{:S(2)}) %collective-permute-start.18) | collective-permute-done | bytes 131104 | tf_op jit(solution)/shard_map/ppermute | solution.py:318
  89.8 0.1 collective-permute-start.19
  89.9 1.8 collective-permute-start.20
  91.8 2.5 %collective-permute-start.21 = (f32[2,2,64,128]{3,2,1,0:T(8,128)S(1)}, f32[2,2,64,128]{3,2,1,0:T(8,128)S(1)}, u32[]{:S(2)}, u32[]{:S(2)}) collective-permute-start(f32[2,2,64,128]{3,2,1,0:T(8,128)S(1)} %select_select_fusion.1), channel_id=1, source_target_pairs={{0,24},{8,16},{16,8},{24,0},{32,56},{40,48},{48,40},{56,32},{64,88... | collective-permute-start | bytes 393224 | tf_op jit(solution)/shard_map/ppermute | solution.py:326
  94.3 5.2 %collective-permute-done.19 = f32[2,2,64,128]{3,2,1,0:T(8,128)S(1)} collective-permute-done((f32[2,2,64,128]{3,2,1,0:T(8,128)S(1)}, f32[2,2,64,128]{3,2,1,0:T(8,128)S(1)}, u32[]{:S(2)}, u32[]{:S(2)}) %collective-permute-start.19) | collective-permute-done | bytes 131104 | tf_op jit(solution)/shard_map/ppermute | solution.py:326
  99.5 2.2 %collective-permute-done.20 = f32[2,2,64,128]{3,2,1,0:T(8,128)S(1)} collective-permute-done((f32[2,2,64,128]{3,2,1,0:T(8,128)S(1)}, f32[2,2,64,128]{3,2,1,0:T(8,128)S(1)}, u32[]{:S(2)}, u32[]{:S(2)}) %collective-permute-start.20) | collective-permute-done | bytes 131104 | tf_op jit(solution)/shard_map/ppermute | solution.py:326
  101.7 6.1 %collective-permute-done.21 = f32[2,2,64,128]{3,2,1,0:T(8,128)S(1)} collective-permute-done((f32[2,2,64,128]{3,2,1,0:T(8,128)S(1)}, f32[2,2,64,128]{3,2,1,0:T(8,128)S(1)}, u32[]{:S(2)}, u32[]{:S(2)}) %collective-permute-start.21) | collective-permute-done | bytes 131104 | tf_op jit(solution)/shard_map/ppermute | solution.py:326
  107.9 0.0 copy-start.2
  107.9 0.3 collective-permute-start.22
  108.2 0.6 pad_add_fusion.where_ref
  108.8 1.4 collective-permute-done.22.other_ref
  110.2 0.0 copy-done.2
  110.2 26.9 %first_half.1 = (f32[512,512]{1,0:T(8,128)}, f32[512,512]{1,0:T(8,128)}) custom-call(s32[4]{0:T(128)} %pad_add_fusion.where_ref, f32[4,2,2,64,128]{4,3,2,1,0:T(8,128)} %copy-done.2, f32[4,2,2,64,128]{4,3,2,1,0:T(8,128)} %collective-permute-done.22.other_ref), custom_call_target="tpu_custom_call" | custom-call | tf_op jit(solution)/shard_map/first_half/pallas_call | solution.py:150
  137.1 0.0 collective-permute-done.15.other_ref
  137.1 1.0 copy-done.3
  138.1 37.7 %second_half.1 = (f32[1024,1024]{1,0:T(8,128)}, f32[1024,1024]{1,0:T(8,128)}) custom-call(s32[4]{0:T(128)} %pad_add_fusion.where_ref, f32[4,2,4,64,128]{4,3,2,1,0:T(8,128)} %copy-done, f32[4,2,4,64,128]{4,3,2,1,0:T(8,128)} %copy-done.3, f32[512,512]{1,0:T(8,128)} %get-tuple-element.12.ua_ref, f32[512,512]{1,0:T(8,128)} %get-tuple-element.13.wa_ref), custom_call_target="tpu_custom_call" | custom-call | tf_op jit(solution)/shard_map/second_half/pallas_call | solution.py:180
  175.7 0.0 collective-permute-done.4.other_ref
  175.7 9.1 %row_factor.1 = (bf16[384,1024]{1,0:T(8,128)(2,1)}, bf16[384,1024]{1,0:T(8,128)(2,1)}, f32[384,128]{1,0:T(8,128)}) custom-call(s32[4]{0:T(128)} %pad_add_fusion.where_ref, f32[4,384,128]{2,1,0:T(8,128)} %copy-done.1, f32[4,384,128]{2,1,0:T(8,128)} %collective-permute-done.4.other_ref, f32[1024,1024]{1,0:T(8,128)} %get-tuple-element.14.u_ref, ...), custom_call_target="tpu_custom_call" | custom-call | tf_op jit(solution)/shard_map/row_factor/pallas_call | solution.py:220
  184.9 10.5 %trailing.1 = f32[4608,128]{1,0:T(8,128)} custom-call(s32[4]{0:T(128)} %pad_add_fusion.where_ref, f32[4608,128]{1,0:T(8,128)} %bitcast.37, f32[32,384,128]{2,1,0:T(8,128)} %bitcast.35, bf16[384,1024]{1,0:T(8,128)(2,1)} %get-tuple-element.16.high_ref, bf16[384,1024]{1,0:T(8,128)(2,1)} %get-tuple-element.17.low_ref, f32[384,128]{1,0:T(8,128)} %get-tuple-element.18.slab_ref), custom_call_target="tpu_custom_call" | custom-call | tf_op jit(solution)/shard_map/trailing/pallas_call | solution.py:269
  (18 shorter events, 0.2 us)
Async XLA Ops:
  6.5 178.3 %all-gather.3.cloned.1.call-start = ((), (), s32[]{:S(2)}) async-start(), calls=%async_computation | async-start | bytes 6488064 | tf_op jit(solution)/shard_map/all_gather | solution.py:312
  7.6 8.8 %collective-permute-start = (f32[384,128]{1,0:T(8,128)S(1)}, f32[384,128]{1,0:T(8,128)S(1)}, u32[]{:S(2)}, u32[]{:S(2)}) collective-permute-start(f32[384,128]{1,0:T(8,128)S(1)} %bitcast.47), channel_id=1, source_target_pairs={{0,192},{8,200},{16,208},{24,216},{32,224},{40,232},{48,240},{56,2... | collective-permute-start | bytes 589832 | tf_op jit(solution)/shard_map/ppermute | solution.py:311
  18.8 5.0 %collective-permute-start.5 = (f32[64,128]{1,0:T(8,128)S(1)}, f32[64,128]{1,0:T(8,128)S(1)}, u32[]{:S(2)}, u32[]{:S(2)}) collective-permute-start(f32[64,128]{1,0:T(8,128)S(1)} %slice.32), channel_id=1, source_target_pairs={{0,6},{1,7},{2,0},{3,1},{4,2},{5,3},{6,4},{7,5},{8,14},{9,15},{10,... | collective-permute-start | bytes 98312 | tf_op jit(solution)/shard_map/ppermute | solution.py:306
  19.4 5.4 %collective-permute-start.6 = (f32[64,128]{1,0:T(8,128)S(1)}, f32[64,128]{1,0:T(8,128)S(1)}, u32[]{:S(2)}, u32[]{:S(2)}) collective-permute-start(f32[64,128]{1,0:T(8,128)S(1)} %slice.32), channel_id=1, source_target_pairs={{0,4},{1,5},{2,6},{3,7},{4,0},{5,1},{6,2},{7,3},{8,12},{9,13},{10,... | collective-permute-start | bytes 98312 | tf_op jit(solution)/shard_map/ppermute | solution.py:306
  21.9 3.9 %collective-permute-start.7 = (f32[64,128]{1,0:T(8,128)S(1)}, f32[64,128]{1,0:T(8,128)S(1)}, u32[]{:S(2)}, u32[]{:S(2)}) collective-permute-start(f32[64,128]{1,0:T(8,128)S(1)} %slice.32), channel_id=1, source_target_pairs={{0,2},{1,3},{2,4},{3,5},{4,6},{5,7},{6,0},{7,1},{8,10},{9,11},{10,... | collective-permute-start | bytes 98312 | tf_op jit(solution)/shard_map/ppermute | solution.py:306
  25.9 11.6 %collective-permute-start.8 = (f32[4,64,128]{2,1,0:T(8,128)S(1)}, f32[4,64,128]{2,1,0:T(8,128)S(1)}, u32[]{:S(2)}, u32[]{:S(2)}) collective-permute-start(f32[4,64,128]{2,1,0:T(8,128)S(1)} %constant_dynamic-slice_fusion), channel_id=1, source_target_pairs={{0,32},{8,40},{16,48},{24,56},{32,0},{40,8},{48,16},{56,24},{64,96... | collective-permute-start | bytes 393224 | tf_op jit(solution)/shard_map/ppermute | solution.py:314
  37.6 2.7 %collective-permute-start.10 = (f32[2,4,64,128]{3,2,1,0:T(8,128)S(1)}, f32[2,4,64,128]{3,2,1,0:T(8,128)S(1)}, u32[]{:S(2)}, u32[]{:S(2)}) collective-permute-start(f32[2,4,64,128]{3,2,1,0:T(8,128)S(1)} %maximum_select_fusion), channel_id=1, source_target_pairs={{64,128},{72,136},{80,144},{88,152},{96,160},{104,168},{112,176},{... | collective-permute-start | bytes 786440 | tf_op jit(solution)/shard_map/ppermute | solution.py:318
  38.3 11.1 %collective-permute-start.11 = (f32[2,4,64,128]{3,2,1,0:T(8,128)S(1)}, f32[2,4,64,128]{3,2,1,0:T(8,128)S(1)}, u32[]{:S(2)}, u32[]{:S(2)}) collective-permute-start(f32[2,4,64,128]{3,2,1,0:T(8,128)S(1)} %maximum_select_fusion), channel_id=1, source_target_pairs={{64,0},{72,8},{80,16},{88,24},{96,32},{104,40},{112,48},{120,56},{... | collective-permute-start | bytes 786440 | tf_op jit(solution)/shard_map/ppermute | solution.py:318
  39.6 9.8 %collective-permute-start.9 = (f32[2,4,64,128]{3,2,1,0:T(8,128)S(1)}, f32[2,4,64,128]{3,2,1,0:T(8,128)S(1)}, u32[]{:S(2)}, u32[]{:S(2)}) collective-permute-start(f32[2,4,64,128]{3,2,1,0:T(8,128)S(1)} %maximum_select_fusion), channel_id=1, source_target_pairs={{64,192},{72,200},{80,208},{88,216},{96,224},{104,232},{112,240},{... | collective-permute-start | bytes 786440 | tf_op jit(solution)/shard_map/ppermute | solution.py:318
  49.4 9.8 %collective-permute-start.12 = (f32[2,4,64,128]{3,2,1,0:T(8,128)S(1)}, f32[2,4,64,128]{3,2,1,0:T(8,128)S(1)}, u32[]{:S(2)}, u32[]{:S(2)}) collective-permute-start(f32[2,4,64,128]{3,2,1,0:T(8,128)S(1)} %select_select_fusion), channel_id=1, source_target_pairs={{0,8},{8,0},{16,24},{24,16},{32,40},{40,32},{48,56},{56,48},{64,72... | collective-permute-start | bytes 786440 | tf_op jit(solution)/shard_map/ppermute | solution.py:326
  50.6 20.8 %collective-permute-start.13 = (f32[2,4,64,128]{3,2,1,0:T(8,128)S(1)}, f32[2,4,64,128]{3,2,1,0:T(8,128)S(1)}, u32[]{:S(2)}, u32[]{:S(2)}) collective-permute-start(f32[2,4,64,128]{3,2,1,0:T(8,128)S(1)} %select_select_fusion), channel_id=1, source_target_pairs={{0,16},{8,24},{16,0},{24,8},{32,48},{40,56},{48,32},{56,40},{64,80... | collective-permute-start | bytes 786440 | tf_op jit(solution)/shard_map/ppermute | solution.py:326
  53.3 25.8 %collective-permute-start.14 = (f32[2,4,64,128]{3,2,1,0:T(8,128)S(1)}, f32[2,4,64,128]{3,2,1,0:T(8,128)S(1)}, u32[]{:S(2)}, u32[]{:S(2)}) collective-permute-start(f32[2,4,64,128]{3,2,1,0:T(8,128)S(1)} %select_select_fusion), channel_id=1, source_target_pairs={{0,24},{8,16},{16,8},{24,0},{32,56},{40,48},{48,40},{56,32},{64,88... | collective-permute-start | bytes 786440 | tf_op jit(solution)/shard_map/ppermute | solution.py:326
  54.1 26.4 %collective-permute-start.2 = (f32[384,128]{1,0:T(8,128)S(1)}, f32[384,128]{1,0:T(8,128)}, u32[]{:S(2)}, u32[]{:S(2)}) collective-permute-start(f32[384,128]{1,0:T(8,128)S(1)} %slice.29), channel_id=1, source_target_pairs={{0,4},{1,5},{2,6},{3,7},{4,0},{5,1},{6,2},{7,3},{8,12},{9,13},{10,... | collective-permute-start | bytes 589832 | tf_op jit(solution)/shard_map/ppermute | solution.py:334
  56.0 25.8 %collective-permute-start.3 = (f32[384,128]{1,0:T(8,128)S(1)}, f32[384,128]{1,0:T(8,128)}, u32[]{:S(2)}, u32[]{:S(2)}) collective-permute-start(f32[384,128]{1,0:T(8,128)S(1)} %slice.29), channel_id=1, source_target_pairs={{0,6},{1,7},{2,0},{3,1},{4,2},{5,3},{6,4},{7,5},{8,14},{9,15},{10,... | collective-permute-start | bytes 589832 | tf_op jit(solution)/shard_map/ppermute | solution.py:334
  59.2 22.7 %collective-permute-start.1 = (f32[384,128]{1,0:T(8,128)S(1)}, f32[384,128]{1,0:T(8,128)}, u32[]{:S(2)}, u32[]{:S(2)}) collective-permute-start(f32[384,128]{1,0:T(8,128)S(1)} %slice.29), channel_id=1, source_target_pairs={{0,2},{1,3},{2,4},{3,5},{4,6},{5,7},{6,0},{7,1},{8,10},{9,11},{10,... | collective-permute-start | bytes 589832 | tf_op jit(solution)/shard_map/ppermute | solution.py:334
  71.4 12.8 %collective-permute-start.16 = (f32[2,2,64,128]{3,2,1,0:T(8,128)S(1)}, f32[2,2,64,128]{3,2,1,0:T(8,128)S(1)}, u32[]{:S(2)}, u32[]{:S(2)}) collective-permute-start(f32[2,2,64,128]{3,2,1,0:T(8,128)S(1)} %slice.33), channel_id=1, source_target_pairs={{0,192},{8,200},{16,208},{24,216},{32,224},{40,232},{48,240},{56,2... | collective-permute-start | bytes 393224 | tf_op jit(solution)/shard_map/ppermute | solution.py:318
  79.0 6.5 %collective-permute-start.17 = (f32[2,2,64,128]{3,2,1,0:T(8,128)S(1)}, f32[2,2,64,128]{3,2,1,0:T(8,128)S(1)}, u32[]{:S(2)}, u32[]{:S(2)}) collective-permute-start(f32[2,2,64,128]{3,2,1,0:T(8,128)S(1)} %slice.33), channel_id=1, source_target_pairs={{0,128},{8,136},{16,144},{24,152},{32,160},{40,168},{48,176},{56,1... | collective-permute-start | bytes 393224 | tf_op jit(solution)/shard_map/ppermute | solution.py:318
  80.5 56.7 %copy-start = (f32[4,2,4,64,128]{4,3,2,1,0:T(8,128)}, f32[4,2,4,64,128]{4,3,2,1,0:T(8,128)S(1)}, u32[]{:S(2)}) copy-start(f32[4,2,4,64,128]{4,3,2,1,0:T(8,128)S(1)} %pad_maximum_fusion.own_ref) | copy-start | bytes 3145732
  80.5 9.3 %collective-permute-start.18 = (f32[2,2,64,128]{3,2,1,0:T(8,128)S(1)}, f32[2,2,64,128]{3,2,1,0:T(8,128)S(1)}, u32[]{:S(2)}, u32[]{:S(2)}) collective-permute-start(f32[2,2,64,128]{3,2,1,0:T(8,128)S(1)} %slice.33), channel_id=1, source_target_pairs={{0,64},{8,72},{16,80},{24,88},{32,96},{40,104},{48,112},{56,120},{... | collective-permute-start | bytes 393224 | tf_op jit(solution)/shard_map/ppermute | solution.py:318
  81.8 55.3 %collective-permute-start.15 = (f32[4,2,4,64,128]{4,3,2,1,0:T(8,128)S(1)}, f32[4,2,4,64,128]{4,3,2,1,0:T(8,128)S(1)}, u32[]{:S(2)}, u32[]{:S(2)}) collective-permute-start(f32[4,2,4,64,128]{4,3,2,1,0:T(8,128)S(1)} %pad_maximum_fusion.own_ref), channel_id=1, source_target_pairs={{0,1},{1,0},{2,3},{3,2},{4,5},{5,4},{6,7},{7,6},{8,9},{9,8},{10,11... | collective-permute-start | bytes 3145736 | tf_op jit(solution)/shard_map/ppermute | solution.py:289
  83.1 92.7 %copy-start.1 = (f32[4,384,128]{2,1,0:T(8,128)}, f32[4,384,128]{2,1,0:T(8,128)S(1)}, u32[]{:S(2)}) copy-start(f32[4,384,128]{2,1,0:T(8,128)S(1)} %pad_maximum_fusion.1.own_ref) | copy-start | bytes 2359300
  83.1 92.7 %collective-permute-start.4 = (f32[4,384,128]{2,1,0:T(8,128)S(1)}, f32[4,384,128]{2,1,0:T(8,128)}, u32[]{:S(2)}, u32[]{:S(2)}) collective-permute-start(f32[4,384,128]{2,1,0:T(8,128)S(1)} %pad_maximum_fusion.1.own_ref), channel_id=1, source_target_pairs={{0,1},{1,0},{2,3},{3,2},{4,5},{5,4},{6,7},{7,6},{8,9},{9,8},{10,11... | collective-permute-start | bytes 2359304 | tf_op jit(solution)/shard_map/ppermute | solution.py:289
  89.8 9.6 %collective-permute-start.19 = (f32[2,2,64,128]{3,2,1,0:T(8,128)S(1)}, f32[2,2,64,128]{3,2,1,0:T(8,128)S(1)}, u32[]{:S(2)}, u32[]{:S(2)}) collective-permute-start(f32[2,2,64,128]{3,2,1,0:T(8,128)S(1)} %select_select_fusion.1), channel_id=1, source_target_pairs={{0,8},{8,0},{16,24},{24,16},{32,40},{40,32},{48,56},{56,48},{64,72... | collective-permute-start | bytes 393224 | tf_op jit(solution)/shard_map/ppermute | solution.py:326
  89.9 11.7 %collective-permute-start.20 = (f32[2,2,64,128]{3,2,1,0:T(8,128)S(1)}, f32[2,2,64,128]{3,2,1,0:T(8,128)S(1)}, u32[]{:S(2)}, u32[]{:S(2)}) collective-permute-start(f32[2,2,64,128]{3,2,1,0:T(8,128)S(1)} %select_select_fusion.1), channel_id=1, source_target_pairs={{0,16},{8,24},{16,0},{24,8},{32,48},{40,56},{48,32},{56,40},{64,80... | collective-permute-start | bytes 393224 | tf_op jit(solution)/shard_map/ppermute | solution.py:326
  91.8 16.1 %collective-permute-start.21 = (f32[2,2,64,128]{3,2,1,0:T(8,128)S(1)}, f32[2,2,64,128]{3,2,1,0:T(8,128)S(1)}, u32[]{:S(2)}, u32[]{:S(2)}) collective-permute-start(f32[2,2,64,128]{3,2,1,0:T(8,128)S(1)} %select_select_fusion.1), channel_id=1, source_target_pairs={{0,24},{8,16},{16,8},{24,0},{32,56},{40,48},{48,40},{56,32},{64,88... | collective-permute-start | bytes 393224 | tf_op jit(solution)/shard_map/ppermute | solution.py:326
  107.9 2.3 %copy-start.2 = (f32[4,2,2,64,128]{4,3,2,1,0:T(8,128)}, f32[4,2,2,64,128]{4,3,2,1,0:T(8,128)S(1)}, u32[]{:S(2)}) copy-start(f32[4,2,2,64,128]{4,3,2,1,0:T(8,128)S(1)} %pad_maximum_fusion.2.own_ref) | copy-start | bytes 1572868
  107.9 2.3 %collective-permute-start.22 = (f32[4,2,2,64,128]{4,3,2,1,0:T(8,128)S(1)}, f32[4,2,2,64,128]{4,3,2,1,0:T(8,128)}, u32[]{:S(2)}, u32[]{:S(2)}) collective-permute-start(f32[4,2,2,64,128]{4,3,2,1,0:T(8,128)S(1)} %pad_maximum_fusion.2.own_ref), channel_id=1, source_target_pairs={{0,1},{1,0},{2,3},{3,2},{4,5},{5,4},{6,7},{7,6},{8,9},{9,8},{10,11... | collective-permute-start | bytes 1572872 | tf_op jit(solution)/shard_map/ppermute | solution.py:289
  137.1 1.0 copy-start.3
Sparse Core Ops, SparseCore 0:
  17.3 106.7 all-gather.2
